TPU v7x, 32 devices: a whole 2x2x4 slice. The times are simulated.
32 devices in a mesh: tok: 8 (over z, y), wid: 4 (over x, core).
Axes of the slice: x: 2, y: 2, z: 4, core: 2. Of those that a mesh axis runs over, the one named last changes fastest.
Arguments:
- queries: bfloat16 [1024, 8192], P('tok', 'wid'), may hold values from -6 to 6
- key_branch: bfloat16 [1024, 8192], P('tok', 'wid'), may hold values from -6 to 6
- value_branch: bfloat16 [1024, 8192], P('tok', 'wid'), may hold values from -6 to 6
- filters: float32 [512, 128], P('wid'), may hold values from -0.5 to 0.5
- out_weight: bfloat16 [8192, 8192], P(None, 'wid'), may hold values from -0.09375 to 0.09375
- cotangent: bfloat16 [1024, 8192], P('tok', 'wid'), may hold values from -6 to 6
Outputs:
- layer_out: bfloat16 [1024, 8192], P('tok', 'wid')
- grad_queries: bfloat16 [1024, 8192], P('tok', 'wid')
- grad_keys: bfloat16 [1024, 8192], P('tok', 'wid')
- grad_values: bfloat16 [1024, 8192], P('tok', 'wid')
- grad_filters: float32 [512, 128], P('wid')
All inputs are finite; a program needn't handle non-finite values.
Results may differ from a plain program's by a relative error of at most 0.02.
Values may be sent and summed in bfloat16 or wider, within the bound.
A program may use at most 192 MiB of HBM per device.

v0:
```python
import functools
import math

import jax
import jax.numpy as jnp
from jax import lax
from jax.experimental import pallas as pl
from jax.experimental.pallas import tpu as pltpu
from jax.sharding import PartitionSpec as P


def iota(shape, dim):
    return lax.broadcasted_iota(jnp.int32, shape, dim)


def circulant(row, kernel):
    return pltpu.roll(jnp.broadcast_to(row, (kernel, kernel)), 0, 1, stride=1, stride_axis=0)


def as_mask(condition):
    return jnp.where(condition, 1.0, 0.0).astype(jnp.bfloat16)


def conv_tile(filters, data, now, group_size, now_first):
    groups, kernel = filters.shape
    tile = data.shape[1]
    inside, outside = as_mask(now), as_mask(jnp.logical_not(now))
    owner = iota((kernel, tile), 1) // group_size
    result = jnp.zeros((kernel, tile), jnp.float32)
    for g in range(groups):
        ring = circulant(filters[g : g + 1], kernel).astype(jnp.bfloat16)
        pair = [ring * inside, ring * outside] if now_first else [ring * outside, ring * inside]
        part = jnp.dot(jnp.concatenate(pair, axis=1), data, preferred_element_type=jnp.float32)
        result = jnp.where(owner == g, part, result)
    return result


def forward_tile(filters_rev, extended, group_size):
    kernel = filters_rev.shape[1]
    now = iota((kernel, kernel), 1) <= iota((kernel, kernel), 0)
    return conv_tile(filters_rev, extended, now, group_size, False)


def backward_tile(filters, grads, group_size):
    kernel = filters.shape[1]
    now = iota((kernel, kernel), 0) <= iota((kernel, kernel), 1)
    return conv_tile(filters, grads, now, group_size, True)


def filter_tile(extended, own_grads, groups, group_size):
    kernel, tile = own_grads.shape
    row, lane = iota((kernel, kernel), 0), iota((kernel, kernel), 1)
    now = row + lane <= kernel - 1
    owner = iota((kernel, tile), 1) // group_size
    mirrored = jnp.dot(
        as_mask(row + lane == kernel - 1), own_grads, preferred_element_type=jnp.float32
    ).astype(jnp.bfloat16)
    rows = []
    for g in range(groups):
        part = lax.dot_general(
            mirrored * as_mask(owner == g),
            extended,
            (((1,), (1,)), ((), ())),
            preferred_element_type=jnp.float32,
        )
        square = jnp.where(now, part[:, kernel:], part[:, :kernel])
        aligned = pltpu.roll(square, 1, 1, stride=1, stride_axis=0)
        rows.append(jnp.sum(aligned, axis=0, keepdims=True))
    return jnp.concatenate(rows, axis=0)


def kernel(
    sizes,
    q_ref, k_ref, v_ref, f_ref, w_ref, cot_ref,
    out_ref, gq_ref, own_out, next_out, gf_ref,
    w_buf, kv_buf, rim_buf, conv_buf, part_buf, sib_out, sib_in, pre_out, pre_in,
    gather, total, gc_buf, gcn_buf, frev_buf, local_buf, terms_buf, all_buf,
    w_sem, kv_send, kv_recv, sib_send, sib_recv, pre_send, pre_recv,
    own_send, own_recv, peer_send, peer_recv, fwd_send, fwd_recv, gc_send, gc_recv,
    term_send, term_recv, sum_send, sum_recv,
):
    n_tok, n_wid, tile, chunk, halves, owners = sizes
    length, width = q_ref.shape
    groups, kernel_size = f_ref.shape
    group_size = width // groups
    tile_groups = tile // group_size
    half = width // halves
    per_piece = half // chunk
    chips = n_wid // 2
    rows = groups // owners
    tok, me = lax.axis_index("tok"), lax.axis_index("wid")
    chip, core = me // 2, lax.rem(me, 2)
    sibling = chip * 2 + 1 - core
    other_chips = [lax.rem(chip + off, chips) for off in range(1, chips)]
    other_toks = [lax.rem(tok + off, n_tok) for off in range(1, n_tok)]
    order = []
    for p in other_chips + [chip]:
        for h in range(halves):
            order += [(p, p * 2 + 1 - core, h), (p, p * 2 + core, h)]

    def w_copy(position, j):
        start = order[position][1] * width + order[position][2] * half + j * chunk
        at = pl.ds(pl.multiple_of(start, chunk), chunk)
        return pltpu.make_async_copy(w_ref.at[at], w_buf.at[at], w_sem.at[position * per_piece + j])

    for position in range(len(order)):
        for j in range(per_piece):
            w_copy(position, j).start()

    def remote(src, dst, send, recv, **where):
        return pltpu.make_async_remote_copy(
            src_ref=src, dst_ref=dst, send_sem=send, recv_sem=recv,
            device_id=where, device_id_type=pl.DeviceIdType.MESH,
        )

    barrier = pltpu.get_barrier_semaphore()
    for where in (
        [{"wid": sibling}] + [{"wid": p * 2 + core} for p in other_chips] + [{"tok": t} for t in other_toks]
    ):
        pl.semaphore_signal(barrier, inc=1, device_id=where, device_id_type=pl.DeviceIdType.MESH)
    pl.semaphore_wait(barrier, 1 + len(other_chips) + len(other_toks))

    kv_buf[...] = (k_ref[...].astype(jnp.float32) * v_ref[...].astype(jnp.float32)).astype(jnp.bfloat16)
    kv_copy = remote(kv_buf, rim_buf, kv_send, kv_recv, tok=lax.rem(tok + 1, n_tok))
    has_next, has_previous = tok < n_tok - 1, tok > 0

    @pl.when(has_next)
    def _():
        kv_copy.start()

    cot = cot_ref[...]

    def sib_copy(p, h):
        at, sem = pl.ds(h * half, half), p * halves + h
        return remote(sib_out.at[p, :, at], sib_in.at[p, :, at], sib_send.at[sem], sib_recv.at[sem], wid=sibling)

    def pre_copy(p, slot, h):
        at = pl.ds(h * half, half)
        return remote(
            pre_out.at[p, :, at], pre_in.at[slot, :, at],
            pre_send.at[p * halves + h], pre_recv.at[slot * halves + h], wid=p * 2 + core,
        )

    def send_sum(p, h):
        at = pl.ds(h * half, half)
        sib_copy(p, h).wait_recv()
        pre_out[p, :, at] = (part_buf[:, at] + sib_in[p, :, at].astype(jnp.float32)).astype(jnp.bfloat16)
        pre_copy(p, chip, h).start()

    waiting = None
    for position, (p, block, h) in enumerate(order):

        @pl.loop(0, per_piece)
        def _(j):
            w_copy(position, j).wait()
            at = pl.ds(pl.multiple_of(block * width + h * half + j * chunk, chunk), chunk)
            part_buf[:, pl.ds(pl.multiple_of(h * half + j * chunk, chunk), chunk)] = lax.dot_general(
                cot, w_buf[at, :], (((1,), (1,)), ((), ())), preferred_element_type=jnp.float32
            )

        if position % 2 == 0:
            at = pl.ds(h * half, half)
            sib_out[p, :, at] = part_buf[:, at].astype(jnp.bfloat16)
            sib_copy(p, h).start()
            if waiting is not None:
                send_sum(*waiting)
                waiting = None
        elif position < 2 * halves * (chips - 1):
            waiting = (p, h)

    flip = jnp.where(
        lax.rem(iota((kernel_size, kernel_size), 0) + iota((kernel_size, kernel_size), 1), kernel_size) == 0, 1.0, 0.0
    ).astype(jnp.bfloat16)
    frev_buf[...] = jnp.dot(f_ref[...].astype(jnp.bfloat16), flip, preferred_element_type=jnp.float32)

    @pl.when(has_previous)
    def _():
        kv_copy.wait_recv()

    @pl.when(jnp.logical_not(has_previous))
    def _():
        rim_buf[...] = jnp.zeros_like(rim_buf)

    def own_copy(h, slot):
        at = pl.ds(h * half, half)
        return remote(gather.at[me, :, at], gather.at[slot, :, at], own_send.at[h], own_recv.at[h], wid=sibling)

    def peer_copy(p, h, slot, slot_chip):
        at = pl.ds(h * half, half)
        return remote(
            gather.at[me, :, at], gather.at[slot, :, at],
            peer_send.at[p * halves + h], peer_recv.at[slot_chip * halves + h], wid=p * 2 + core,
        )

    def fwd_copy(p, h, slot):
        at = pl.ds(h * half, half)
        return remote(
            gather.at[p * 2 + core, :, at], gather.at[slot, :, at],
            fwd_send.at[p * halves + h], fwd_recv.at[p * halves + h], wid=sibling,
        )

    for h in range(halves):

        @pl.loop(h * (half // tile), (h + 1) * (half // tile))
        def _(i):
            at = pl.ds(pl.multiple_of(i * tile, tile), tile)
            which = pl.ds(pl.multiple_of(i * tile_groups, tile_groups), tile_groups)
            extended = jnp.concatenate([rim_buf[:, at], kv_buf[:, at]], axis=0)
            conv = forward_tile(frev_buf[which, :], extended, group_size)
            conv_buf[:, at] = conv
            gather[me, :, at] = (q_ref[:, at].astype(jnp.float32) * conv).astype(jnp.bfloat16)

        for p in other_chips:
            peer_copy(p, h, me, chip).start()
        own_copy(h, me).start()

    for h in range(halves):
        sib_copy(chip, h).wait_recv()
        for p in other_chips:
            pre_copy(p, p, h).wait_recv()

    @pl.loop(0, width // tile)
    def _(i):
        at = pl.ds(pl.multiple_of(i * tile, tile), tile)
        grad_gated = part_buf[:, at] + sib_in[chip, :, at].astype(jnp.float32)
        for p in other_chips:
            grad_gated = grad_gated + pre_in[p, :, at].astype(jnp.float32)
        gc_buf[:, at] = (grad_gated * q_ref[:, at].astype(jnp.float32)).astype(jnp.bfloat16)
        gq_ref[:, at] = (grad_gated * conv_buf[:, at]).astype(jnp.bfloat16)

    gc_copy = remote(gc_buf, gcn_buf, gc_send, gc_recv, tok=lax.rem(tok + n_tok - 1, n_tok))

    @pl.when(has_previous)
    def _():
        gc_copy.start()

    @pl.loop(0, width // tile)
    def _(i):
        at = pl.ds(pl.multiple_of(i * tile, tile), tile)
        which = pl.ds(pl.multiple_of(i * tile_groups, tile_groups), tile_groups)
        extended = jnp.concatenate([rim_buf[:, at], kv_buf[:, at]], axis=0)
        local_buf[which, :] = filter_tile(extended, gc_buf[:, at], tile_groups, group_size)

    local_buf[...] = jnp.dot(
        local_buf[...], flip.astype(jnp.float32), preferred_element_type=jnp.float32, precision=lax.Precision.HIGHEST
    )

    def owned(t):
        return pl.ds(pl.multiple_of(t * rows, rows), rows)

    def term_copy(t, slot):
        return remote(local_buf.at[owned(lax.rem(t, owners))], terms_buf.at[slot], term_send.at[t], term_recv.at[slot], tok=t)

    def sum_copy(t, owner):
        return remote(all_buf.at[owned(owner)], all_buf.at[owned(owner)], sum_send.at[t], sum_recv.at[owner], tok=t)

    def if_owner(t, action):
        if owners == n_tok:
            action()
        else:
            pl.when(t < owners)(action)

    for t in other_toks:
        if_owner(t, lambda t=t: term_copy(t, tok).start())

    def project(block, start, depth, first):
        @pl.loop(0, width // chunk)
        def _(j):
            at = pl.ds(pl.multiple_of(j * chunk, chunk), chunk)
            deep = pl.ds(pl.multiple_of(block * width + start, depth), depth)
            product = jnp.dot(
                gather[block, :, pl.ds(start, depth)], w_buf[deep, at], preferred_element_type=jnp.float32
            )
            total[:, at] = product if first else total[:, at] + product

    project(me, 0, width, True)
    for h in range(halves):
        own_copy(h, sibling).wait_recv()

    def sum_terms():
        for t in other_toks:
            term_copy(t, t).wait_recv()
        terms_buf[tok] = local_buf[owned(tok), :]
        all_buf[owned(tok), :] = jnp.sum(terms_buf[...], axis=0)
        for t in other_toks:
            sum_copy(t, tok).start()

    for h in range(halves):
        for p in other_chips:
            peer_copy(p, h, p * 2 + core, p).wait_recv()
            fwd_copy(p, h, p * 2 + core).start()
    project(sibling, 0, width, False)
    for p in other_chips:
        project(p * 2 + core, 0, width, False)
    if_owner(tok, sum_terms)
    for p in other_chips:
        for h in range(halves):
            fwd_copy(p, h, p * 2 + 1 - core).wait_recv()
        project(p * 2 + 1 - core, 0, width, False)
    out_ref[...] = total[...].astype(jnp.bfloat16)

    @pl.when(has_next)
    def _():
        gc_copy.wait_recv()

    @pl.when(jnp.logical_not(has_next))
    def _():
        gcn_buf[...] = jnp.zeros_like(gcn_buf)

    own_out[...] = gc_buf[...]
    next_out[...] = gcn_buf[...]
    for t in other_toks:
        if_owner(t, lambda t=t: sum_copy(t, t).wait_recv())
    gf_ref[...] = all_buf[...]

    pl.when(has_next)(lambda: kv_copy.wait_send())
    pl.when(has_previous)(lambda: gc_copy.wait_send())
    for h in range(halves):
        for p in other_chips + [chip]:
            sib_copy(p, h).wait_send()
        for p in other_chips:
            pre_copy(p, chip, h).wait_send()
    for h in range(halves):
        own_copy(h, me).wait_send()
        for p in other_chips:
            peer_copy(p, h, me, chip).wait_send()
            fwd_copy(p, h, p * 2 + core).wait_send()
    for t in other_toks:
        if_owner(t, lambda t=t: term_copy(t, tok).wait_send())

    def sums_sent():
        for t in other_toks:
            sum_copy(t, tok).wait_send()

    if_owner(tok, sums_sent)


def last_kernel(
    group_size, tile, scale, out_ref, gq_ref, own_ref, next_ref, sums_ref, k_ref, v_ref, f_ref,
    out, gq, gk, gv, gf,
):
    out[...] = out_ref[...]
    gq[...] = gq_ref[...]
    gf[...] = sums_ref[...] * scale
    tile_groups = tile // group_size

    @pl.loop(0, k_ref.shape[1] // tile)
    def _(i):
        at = pl.ds(pl.multiple_of(i * tile, tile), tile)
        which = pl.ds(pl.multiple_of(i * tile_groups, tile_groups), tile_groups)
        grads = jnp.concatenate([own_ref[:, at], next_ref[:, at]], axis=0)
        grad_kv = backward_tile(f_ref[which, :], grads, group_size)
        gk[:, at] = (grad_kv * v_ref[:, at].astype(jnp.float32)).astype(jnp.bfloat16)
        gv[:, at] = (grad_kv * k_ref[:, at].astype(jnp.float32)).astype(jnp.bfloat16)


def local(queries, key_branch, value_branch, filters, out_weight, cotangent):
    length, width = queries.shape
    groups, kernel_size = filters.shape
    n_tok, n_wid = lax.axis_size("tok"), lax.axis_size("wid")
    chips = n_wid // 2
    group_size = width // groups
    tile, halves = min(128, width // 2), 2
    chunk = min(512, width // halves)
    step = min(512, width)
    owners = min(n_tok, groups // 8)
    bf16, f32 = jnp.bfloat16, jnp.float32
    wide = jax.ShapeDtypeStruct((length, width), bf16)
    dma = pltpu.SemaphoreType.DMA
    vmem = pl.BlockSpec(memory_space=pltpu.VMEM)
    results = pl.pallas_call(
        functools.partial(kernel, (n_tok, n_wid, tile, chunk, halves, owners)),
        in_specs=[vmem] * 4 + [pl.BlockSpec(memory_space=pl.ANY), vmem],
        out_specs=[vmem] * 5,
        out_shape=[wide] * 4 + [jax.ShapeDtypeStruct(filters.shape, f32)],
        scratch_shapes=[
            pltpu.VMEM(out_weight.shape, bf16),
            pltpu.VMEM((length, width), bf16),
            pltpu.VMEM((length, width), bf16),
            pltpu.VMEM((length, width), f32),
            pltpu.VMEM((length, width), f32),
            pltpu.VMEM((chips, length, width), bf16),
            pltpu.VMEM((chips, length, width), bf16),
            pltpu.VMEM((chips, length, width), bf16),
            pltpu.VMEM((chips, length, width), bf16),
            pltpu.VMEM((n_wid, length, width), bf16),
            pltpu.VMEM((length, width), f32),
            pltpu.VMEM((length, width), bf16),
            pltpu.VMEM((length, width), bf16),
            pltpu.VMEM(filters.shape, f32),
            pltpu.VMEM(filters.shape, f32),
            pltpu.VMEM((n_tok, groups // owners, kernel_size), f32),
            pltpu.VMEM(filters.shape, f32),
            dma((n_wid * (width // chunk),)),
            dma, dma,
            dma((chips * halves,)), dma((chips * halves,)), dma((chips * halves,)), dma((chips * halves,)),
            dma((halves,)), dma((halves,)),
            dma((chips * halves,)), dma((chips * halves,)), dma((chips * halves,)), dma((chips * halves,)),
            dma, dma,
            dma((n_tok,)), dma((n_tok,)), dma((n_tok,)), dma((n_tok,)),
        ],
        compiler_params=pltpu.CompilerParams(
            collective_id=0, has_side_effects=True, vmem_limit_bytes=60 * 2**20
        ),
        cost_estimate=pl.CostEstimate(
            flops=4 * length * width * width * n_wid, bytes_accessed=2 * width * width * n_wid, transcendentals=0
        ),
    )(queries, key_branch, value_branch, filters, out_weight, cotangent)
    channels = pl.BlockSpec((length, step), lambda i: (0, i))
    by_group = pl.BlockSpec((step // group_size, kernel_size), lambda i: (i, 0))
    scale = 1.0 / math.sqrt(length * n_tok * group_size)
    return pl.pallas_call(
        functools.partial(last_kernel, group_size, tile, scale),
        grid=(width // step,),
        in_specs=[channels] * 4 + [by_group, channels, channels, by_group],
        out_specs=[channels] * 4 + [by_group],
        out_shape=[wide] * 4 + [jax.ShapeDtypeStruct(filters.shape, f32)],
    )(*results, key_branch, value_branch, filters)


def solution(mesh):
    return jax.shard_map(
        local,
        mesh=mesh,
        in_specs=(
            P("tok", "wid"),
            P("tok", "wid"),
            P("tok", "wid"),
            P("wid", None),
            P(None, "wid"),
            P("tok", "wid"),
        ),
        out_specs=(
            P("tok", "wid"),
            P("tok", "wid"),
            P("tok", "wid"),
            P("tok", "wid"),
            P("wid", None),
        ),
        check_vma=False,
    )
```

profile of v0, /device:TPU:0, one launch (start us, length us, event | category | flops | bytes accessed | tf_op | source)
XLA Modules:
  0.0 55.4 jit_solution(11057502185539589077)
XLA Ops:
  0.6 46.8 %shard_map.101 = (bf16[128,2048]{1,0:T(8,128)(2,1)}, bf16[128,2048]{1,0:T(8,128)(2,1)}, bf16[128,2048]{1,0:T(8,128)(2,1)}, bf16[128,2048]{1,0:T(8,128)(2,1)}, f32[128,128]{1,0:T(8,128)}) custom-call(bf16[128,2048]{1,0:T(8,128)(2,1)} %q_ref.1, bf16[128,2048]{1,0:T(8,128)(2,1)} %k_ref.3, bf16[128,2048]{1,0:T(8,128)(2,1)} %v_ref.3, f32[128,128]{1,0:T(8,128)} %f_ref.3, ...), custom_call_target="tpu_custom_call" | custom-call | flops 8589934592 | bytes 33554432 | tf_op jit(solution)/shard_map/pallas_call | solution.py:371
  47.5 7.9 %shard_map.102 = (bf16[128,2048]{1,0:T(8,128)(2,1)}, bf16[128,2048]{1,0:T(8,128)(2,1)}, bf16[128,2048]{1,0:T(8,128)(2,1)}, bf16[128,2048]{1,0:T(8,128)(2,1)}, f32[128,128]{1,0:T(8,128)}) custom-call(bf16[128,2048]{1,0:T(8,128)(2,1)} %get-tuple-element.10.out_ref, bf16[128,2048]{1,0:T(8,128)(2,1)} %get-tuple-element.11.gq_ref, ...), custom_call_target="tpu_custom_call" | custom-call | tf_op jit(solution)/shard_map/pallas_call | solution.py:412
where the time goes:
time: 55.6 us; the launch traced here: 55.4 us
  Pallas kernels  54.8 us (99%)
  between operations  0.64 us (1%)
    pallas_call x1, Pallas kernels, local(): pl.pallas_call(functools.partial(kernel, (n_tok, n_wid, tile, chunk, halv...  46.8 us
    pallas_call x1, Pallas kernels, local(): pl.pallas_call(functools.partial(last_kernel, group_size, tile, scale), g...  7.94 us

commit v1 on v0

v1 whole, which is shorter than its diff:
```python
import functools
import math

import jax
import jax.numpy as jnp
from jax import lax
from jax.experimental import pallas as pl
from jax.experimental.pallas import tpu as pltpu
from jax.sharding import PartitionSpec as P

bf16, f32 = jnp.bfloat16, jnp.float32


def iota(shape, dim):
    return lax.broadcasted_iota(jnp.int32, shape, dim)


def as_mask(condition):
    return jnp.where(condition, 1.0, 0.0).astype(bf16)


def dot(a, b):
    return jnp.dot(a, b, preferred_element_type=f32)


def fanned(rows):
    return pltpu.roll(rows, 0, 1, stride=1, stride_axis=0)


def conv_tile(filters, own, other, keep, group_size):
    groups, kernel = filters.shape
    data = jnp.concatenate([own, other], axis=1)
    parts = []
    for g in range(groups):
        ring = fanned(jnp.broadcast_to(filters[g : g + 1], (kernel, kernel))).astype(bf16)
        kept = ring * keep
        taps = jnp.concatenate([kept, ring - kept], axis=0)
        parts.append(dot(data[g * group_size : (g + 1) * group_size], taps))
    return jnp.concatenate(parts, axis=0)


def filter_tile(before, own, grads, mirror, groups, group_size):
    tile, kernel = own.shape
    half = kernel // 2
    window = jnp.concatenate([before, own], axis=1)
    later = jnp.concatenate([window[:, half:], window[:, :half]], axis=1)
    data = jnp.concatenate([window, later], axis=0)
    turned = dot(mirror, grads.T).astype(bf16)
    turned = jnp.concatenate([turned[:half], turned[half:]], axis=1)
    owner = lax.rem(iota((half, 2 * tile), 1), tile) // group_size
    now = iota((half, kernel), 0) + iota((half, kernel), 1) <= half - 1
    rows = []
    for g in range(groups):
        part = dot(turned * as_mask(owner == g), data)
        square = jnp.where(now, part[:, kernel:], part[:, :kernel])
        rows.append(jnp.sum(fanned(square), axis=0, keepdims=True))
    return jnp.concatenate(rows, axis=0)


def kernel(
    sizes, scale,
    q_hbm, k_hbm, v_hbm, f_hbm, w_hbm, cot_hbm,
    out_hbm, gq_hbm, gk_hbm, gv_hbm, gf_hbm,
    q_ref, k_ref, v_ref, f_ref, cot_ref, w_buf, cot_t, q_t, kv_t, rim_t, conv_t, part_t,
    sib_out, sib_in, pre_out, pre_in, gather, total, gc_t, gcn_t,
    out_buf, gq_buf, gk_buf, gv_buf, frev_buf, local_buf, terms_buf, all_buf,
    in_sem, out_sem, w_sem, kv_send, kv_recv, sib_send, sib_recv, pre_send, pre_recv,
    own_send, own_recv, peer_send, peer_recv, fwd_send, fwd_recv, gc_send, gc_recv,
    term_send, term_recv, sum_send, sum_recv,
):
    n_tok, n_wid, tile, piece, owners = sizes
    length, width = q_ref.shape
    groups, kernel_size = f_ref.shape
    group_size = width // groups
    tile_groups = tile // group_size
    pieces = width // piece
    tiles = piece // tile
    chips = n_wid // 2
    steps = (chips - 1) * pieces
    rows = groups // owners
    tok, me = lax.axis_index("tok"), lax.axis_index("wid")
    chip, core = me // 2, lax.rem(me, 2)
    sibling = chip * 2 + 1 - core
    other_chips = [lax.rem(chip + off, chips) for off in range(1, chips)]
    other_toks = [lax.rem(tok + off, n_tok) for off in range(1, n_tok)]
    has_next, has_previous = tok < n_tok - 1, tok > 0

    def step_of(i):
        return lax.rem(chip + 1 + i // pieces, chips), lax.rem(i, pieces)

    def span(h):
        return pl.ds(pl.multiple_of(h * piece, piece), piece)

    def tile_of(h, i):
        return pl.ds(pl.multiple_of(h * piece + i * tile, tile), tile)

    def groups_of(h, i):
        return pl.ds(pl.multiple_of((h * tiles + i) * tile_groups, tile_groups), tile_groups)

    ins = [
        pltpu.make_async_copy(src, dst, in_sem.at[i])
        for i, (src, dst) in enumerate(
            [(k_hbm, k_ref), (v_hbm, v_ref), (cot_hbm, cot_ref), (q_hbm, q_ref), (f_hbm, f_ref)]
        )
    ]
    for copy in ins[:3]:
        copy.start()

    def w_rows(block, h):
        return pl.ds(pl.multiple_of(block * width + h * piece, piece), piece)

    def w_copy(block, h):
        at = w_rows(block, h)
        return pltpu.make_async_copy(w_hbm.at[at], w_buf.at[at], w_sem.at[block * pieces + h])

    @pl.loop(0, steps)
    def _(i):
        p, h = step_of(i)
        w_copy(p * 2 + 1 - core, h).start()
        w_copy(p * 2 + core, h).start()

    for copy in ins[3:]:
        copy.start()
    for block in (sibling, me):

        @pl.loop(0, pieces)
        def _(h):
            w_copy(block, h).start()

    def remote(src, dst, send, recv, **where):
        return pltpu.make_async_remote_copy(
            src_ref=src, dst_ref=dst, send_sem=send, recv_sem=recv,
            device_id=where, device_id_type=pl.DeviceIdType.MESH,
        )

    barrier = pltpu.get_barrier_semaphore()
    for where in (
        [{"wid": sibling}] + [{"wid": p * 2 + core} for p in other_chips] + [{"tok": t} for t in other_toks]
    ):
        pl.semaphore_signal(barrier, inc=1, device_id=where, device_id_type=pl.DeviceIdType.MESH)

    ins[0].wait()
    ins[1].wait()

    @pl.loop(0, pieces)
    def _(h):
        for i in range(tiles):
            at = tile_of(h, i)
            kv_t[at, :] = (k_ref[:, at].astype(f32) * v_ref[:, at].astype(f32)).astype(bf16).T

    ins[2].wait()

    @pl.loop(0, pieces)
    def _(h):
        for i in range(tiles):
            at = tile_of(h, i)
            cot_t[at, :] = cot_ref[:, at].T

    pl.semaphore_wait(barrier, 1 + len(other_chips) + len(other_toks))

    def kv_copy(h):
        return remote(
            kv_t.at[span(h)], rim_t.at[span(h)], kv_send.at[h], kv_recv.at[h], tok=lax.rem(tok + 1, n_tok)
        )

    def gc_copy(h):
        return remote(
            gc_t.at[span(h)], gcn_t.at[span(h)], gc_send.at[h], gc_recv.at[h], tok=lax.rem(tok + n_tok - 1, n_tok)
        )

    @pl.when(has_next)
    def _():
        for h in range(pieces):
            kv_copy(h).start()

    def sib_copy(p, h):
        sem = p * pieces + h
        return remote(
            sib_out.at[p, span(h)], sib_in.at[p, span(h)], sib_send.at[sem], sib_recv.at[sem], wid=sibling
        )

    def pre_copy(p, slot, h):
        return remote(
            pre_out.at[p, span(h)], pre_in.at[slot, span(h)],
            pre_send.at[p * pieces + h], pre_recv.at[slot * pieces + h], wid=p * 2 + core,
        )

    def grad_rows(block, h):
        w_copy(block, h).wait()
        return dot(w_buf[w_rows(block, h), :], cot_t[...])

    def send_sum(i):
        p, h = step_of(i)
        sib_copy(p, h).wait_recv()
        pre_out[p, span(h), :] = (part_t[span(h), :] + sib_in[p, span(h), :].astype(f32)).astype(bf16)
        pre_copy(p, chip, h).start()

    @pl.loop(0, steps)
    def _(i):
        p, h = step_of(i)
        sib_out[p, span(h), :] = grad_rows(p * 2 + 1 - core, h).astype(bf16)
        sib_copy(p, h).start()
        pl.when(i > 0)(lambda: send_sum(i - 1))
        part_t[span(h), :] = grad_rows(p * 2 + core, h)

    @pl.loop(0, pieces)
    def _(h):
        sib_out[chip, span(h), :] = grad_rows(sibling, h).astype(bf16)
        sib_copy(chip, h).start()
        pl.when(h == 0)(lambda: send_sum(steps - 1))

    ins[3].wait()
    ins[4].wait()
    lanes, sublanes = iota((kernel_size, kernel_size), 1), iota((kernel_size, kernel_size), 0)
    flip = as_mask(lax.rem(lanes + sublanes, kernel_size) == 0)
    frev_buf[...] = dot(f_ref[...].astype(bf16), flip)

    def own_copy(h, slot):
        return remote(
            gather.at[me, :, span(h)], gather.at[slot, :, span(h)], own_send.at[h], own_recv.at[h], wid=sibling
        )

    def peer_copy(p, h, slot, slot_chip):
        return remote(
            gather.at[me, :, span(h)], gather.at[slot, :, span(h)],
            peer_send.at[p * pieces + h], peer_recv.at[slot_chip * pieces + h], wid=p * 2 + core,
        )

    def fwd_copy(p, h, slot):
        return remote(
            gather.at[p * 2 + core, :, span(h)], gather.at[slot, :, span(h)],
            fwd_send.at[p * pieces + h], fwd_recv.at[p * pieces + h], wid=sibling,
        )

    @pl.when(jnp.logical_not(has_previous))
    def _():
        rim_t[...] = jnp.zeros_like(rim_t)

    def forward_piece(h):
        @pl.when(has_previous)
        def _():
            kv_copy(h).wait_recv()

        keep = as_mask(sublanes <= lanes)
        for i in range(tiles):
            at = tile_of(h, i)
            turned = q_ref[:, at].T
            conv = conv_tile(f_ref[groups_of(h, i), :], kv_t[at, :], rim_t[at, :], keep, group_size)
            q_t[at, :] = turned
            conv_t[at, :] = conv
            gather[me, :, at] = (turned.astype(f32) * conv).astype(bf16).T
        for p in other_chips:
            peer_copy(p, h, me, chip).start()
        own_copy(h, me).start()

    @pl.loop(0, pieces)
    def _(h):
        forward_piece(h)
        part_t[span(h), :] = grad_rows(me, h)

    mirror = as_mask(
        jnp.logical_and(
            lanes // (kernel_size // 2) == sublanes // (kernel_size // 2),
            lax.rem(lanes, kernel_size // 2) + lax.rem(sublanes, kernel_size // 2) == kernel_size // 2 - 1,
        )
    )

    @pl.loop(0, pieces)
    def _(h):
        sib_copy(chip, h).wait_recv()
        for p in other_chips:
            pre_copy(p, p, h).wait_recv()
        for i in range(tiles):
            at = tile_of(h, i)
            grad_gated = part_t[at, :] + sib_in[chip, at, :].astype(f32)
            for p in other_chips:
                grad_gated = grad_gated + pre_in[p, at, :].astype(f32)
            gc_t[at, :] = (grad_gated * q_t[at, :].astype(f32)).astype(bf16)
            gq_buf[:, at] = (grad_gated * conv_t[at, :]).astype(bf16).T

        @pl.when(has_previous)
        def _():
            gc_copy(h).start()

        for i in range(tiles):
            at = tile_of(h, i)
            local_buf[groups_of(h, i), :] = filter_tile(
                rim_t[at, :], kv_t[at, :], gc_t[at, :], mirror, tile_groups, group_size
            )

    outs = [
        pltpu.make_async_copy(src, dst, out_sem.at[i])
        for i, (src, dst) in enumerate(
            [(gq_buf, gq_hbm), (gk_buf, gk_hbm), (gv_buf, gv_hbm), (out_buf, out_hbm), (all_buf, gf_hbm)]
        )
    ]
    outs[0].start()
    back = jnp.where(
        lax.rem(lanes + sublanes + kernel_size // 2 + 1, kernel_size) == 0, 1.0, 0.0
    ).astype(f32)
    local_buf[...] = jnp.dot(local_buf[...], back, preferred_element_type=f32, precision=lax.Precision.HIGHEST)

    def owned(t):
        return pl.ds(pl.multiple_of(t * rows, rows), rows)

    def term_copy(t, slot):
        return remote(local_buf.at[owned(lax.rem(t, owners))], terms_buf.at[slot], term_send.at[t], term_recv.at[slot], tok=t)

    def sum_copy(t, owner):
        return remote(all_buf.at[owned(owner)], all_buf.at[owned(owner)], sum_send.at[t], sum_recv.at[owner], tok=t)

    def if_owner(t, action):
        if owners == n_tok:
            action()
        else:
            pl.when(t < owners)(action)

    for t in other_toks:
        if_owner(t, lambda t=t: term_copy(t, tok).start())

    def project(block, start, depth, first=False):
        deep = pl.ds(pl.multiple_of(block * width + start, depth), depth)
        product = dot(gather[block, :, pl.ds(pl.multiple_of(start, depth), depth)], w_buf[deep, :])
        total[...] = product if first else total[...] + product

    project(me, 0, width, True)
    for h in range(pieces):
        own_copy(h, sibling).wait_recv()
    project(sibling, 0, width)

    def sum_terms():
        for t in other_toks:
            term_copy(t, t).wait_recv()
        terms_buf[tok] = local_buf[owned(tok), :]
        all_buf[owned(tok), :] = jnp.sum(terms_buf[...], axis=0) * scale
        for t in other_toks:
            sum_copy(t, tok).start()

    if_owner(tok, sum_terms)

    @pl.when(jnp.logical_not(has_next))
    def _():
        gcn_t[...] = jnp.zeros_like(gcn_t)

    @pl.loop(0, pieces)
    def _(h):
        @pl.when(has_next)
        def _():
            gc_copy(h).wait_recv()

        keep = as_mask(lanes <= sublanes)
        for i in range(tiles):
            at = tile_of(h, i)
            grad_kv = conv_tile(frev_buf[groups_of(h, i), :], gc_t[at, :], gcn_t[at, :], keep, group_size).T
            gk_buf[:, at] = (grad_kv * v_ref[:, at].astype(f32)).astype(bf16)
            gv_buf[:, at] = (grad_kv * k_ref[:, at].astype(f32)).astype(bf16)

    outs[1].start()
    outs[2].start()

    def last_half(i):
        p, h = step_of(i)
        fwd_copy(p, h, p * 2 + 1 - core).wait_recv()
        project(p * 2 + 1 - core, h * piece, piece)

    @pl.loop(0, steps)
    def _(i):
        p, h = step_of(i)
        peer_copy(p, h, p * 2 + core, p).wait_recv()
        fwd_copy(p, h, p * 2 + core).start()
        pl.when(i > 0)(lambda: last_half(i - 1))
        project(p * 2 + core, h * piece, piece)

    last_half(steps - 1)
    out_buf[...] = total[...].astype(bf16)
    outs[3].start()
    for t in other_toks:
        if_owner(t, lambda t=t: sum_copy(t, t).wait_recv())
    outs[4].start()

    for h in range(pieces):
        pl.when(has_next)(lambda h=h: kv_copy(h).wait_send())
        pl.when(has_previous)(lambda h=h: gc_copy(h).wait_send())
        sib_copy(chip, h).wait_send()
        own_copy(h, me).wait_send()

    @pl.loop(0, steps)
    def _(i):
        p, h = step_of(i)
        sib_copy(p, h).wait_send()
        pre_copy(p, chip, h).wait_send()
        peer_copy(p, h, me, chip).wait_send()
        fwd_copy(p, h, p * 2 + core).wait_send()

    for t in other_toks:
        if_owner(t, lambda t=t: term_copy(t, tok).wait_send())

    def sums_sent():
        for t in other_toks:
            sum_copy(t, tok).wait_send()

    if_owner(tok, sums_sent)
    for copy in outs:
        copy.wait()


def hand_on(*refs):
    count = len(refs) // 2
    sems = refs[-1]
    copies = [pltpu.make_async_copy(refs[i], refs[count + i], sems.at[i]) for i in range(count)]
    for copy in copies:
        copy.start()
    for copy in copies:
        copy.wait()


def local(queries, key_branch, value_branch, filters, out_weight, cotangent):
    length, width = queries.shape
    groups, kernel_size = filters.shape
    n_tok, n_wid = lax.axis_size("tok"), lax.axis_size("wid")
    chips = n_wid // 2
    group_size = width // groups
    tile = min(128, width // 2)
    piece = max(tile, width // 4)
    pieces = width // piece
    owners = min(n_tok, groups // 8)
    wide = jax.ShapeDtypeStruct((length, width), bf16)
    results = [wide] * 4 + [jax.ShapeDtypeStruct(filters.shape, f32)]
    dma = pltpu.SemaphoreType.DMA
    hbm = pl.BlockSpec(memory_space=pl.ANY)
    flat, turned = pltpu.VMEM((length, width), bf16), pltpu.VMEM((width, length), bf16)
    turned_f32 = pltpu.VMEM((width, length), f32)
    by_chip = pltpu.VMEM((chips, width, length), bf16)
    taps = pltpu.VMEM(filters.shape, f32)
    scale = 1.0 / math.sqrt(length * n_tok * group_size)
    outs = pl.pallas_call(
        functools.partial(kernel, (n_tok, n_wid, tile, piece, owners), scale),
        in_specs=[hbm] * 6,
        out_specs=[hbm] * 5,
        out_shape=results,
        scratch_shapes=[
            flat, flat, flat, taps, flat,
            pltpu.VMEM(out_weight.shape, bf16),
            turned, turned, turned, turned, turned_f32, turned_f32,
            by_chip, by_chip, by_chip, by_chip,
            pltpu.VMEM((n_wid, length, width), bf16),
            pltpu.VMEM((length, width), f32),
            turned, turned,
            flat, flat, flat, flat,
            taps, taps,
            pltpu.VMEM((n_tok, groups // owners, kernel_size), f32),
            taps,
            dma((5,)), dma((5,)), dma((n_wid * pieces,)),
            dma((pieces,)), dma((pieces,)),
            dma((chips * pieces,)), dma((chips * pieces,)), dma((chips * pieces,)), dma((chips * pieces,)),
            dma((pieces,)), dma((pieces,)),
            dma((chips * pieces,)), dma((chips * pieces,)), dma((chips * pieces,)), dma((chips * pieces,)),
            dma((pieces,)), dma((pieces,)),
            dma((n_tok,)), dma((n_tok,)), dma((n_tok,)), dma((n_tok,)),
        ],
        compiler_params=pltpu.CompilerParams(
            collective_id=0, has_side_effects=True, vmem_limit_bytes=60 * 2**20
        ),
        cost_estimate=pl.CostEstimate(
            flops=4 * length * width * width * n_wid, bytes_accessed=2 * width * width * n_wid, transcendentals=0
        ),
    )(queries, key_branch, value_branch, filters, out_weight, cotangent)
    return pl.pallas_call(
        hand_on, in_specs=[hbm] * 5, out_specs=[hbm] * 5, out_shape=results, scratch_shapes=[dma((5,))]
    )(*outs)


def solution(mesh):
    return jax.shard_map(
        local,
        mesh=mesh,
        in_specs=(
            P("tok", "wid"),
            P("tok", "wid"),
            P("tok", "wid"),
            P("wid", None),
            P(None, "wid"),
            P("tok", "wid"),
        ),
        out_specs=(
            P("tok", "wid"),
            P("tok", "wid"),
            P("tok", "wid"),
            P("tok", "wid"),
            P("wid", None),
        ),
        check_vma=False,
    )
```

time: 55.6 us -> 115 us (2.07)
  Pallas kernels: 54.8 us -> 114 us
    pallas_call x2, Pallas kernels: 54.8 us -> 114 us  [the longest x1 66.7 us: local(): pl.pallas_call(hand_on, in_specs=[hbm] * 5, out_specs=[hbm] * 5, out_shap...]
where the time goes in v1:
time: 115 us
  Pallas kernels  114 us (99%)
    pallas_call x1, Pallas kernels, local(): pl.pallas_call(hand_on, in_specs=[hbm] * 5, out_specs=[hbm] * 5, out_shap...  66.7 us
    pallas_call x1, Pallas kernels, local(): pl.pallas_call(functools.partial(kernel, (n_tok, n_wid, tile, piece, owne...  47.5 us

profile of v1, /device:TPU:0, one launch (start us, length us, event | category | flops | bytes accessed | tf_op | source)
XLA Modules:
  0.0 114.8 jit_solution(15918678120216899145)
XLA Ops:
  0.6 47.5 %shard_map.101 = (bf16[128,2048]{1,0:T(8,128)(2,1)}, bf16[128,2048]{1,0:T(8,128)(2,1)}, bf16[128,2048]{1,0:T(8,128)(2,1)}, bf16[128,2048]{1,0:T(8,128)(2,1)}, f32[128,128]{1,0:T(8,128)}) custom-call(bf16[128,2048]{1,0:T(8,128)(2,1)} %q_hbm.1, bf16[128,2048]{1,0:T(8,128)(2,1)} %k_hbm.1, bf16[128,2048]{1,0:T(8,128)(2,1)} %v_hbm.1, f32[128,128]{1,0:T(8,128)} %f_hbm.1, ...), custom_call_target="tpu_custom_call" | custom-call | flops 8589934592 | bytes 33554432 | tf_op jit(solution)/shard_map/pallas_call | solution.py:436
  48.1 66.7 %shard_map.102 = (bf16[128,2048]{1,0:T(8,128)(2,1)}, bf16[128,2048]{1,0:T(8,128)(2,1)}, bf16[128,2048]{1,0:T(8,128)(2,1)}, bf16[128,2048]{1,0:T(8,128)(2,1)}, f32[128,128]{1,0:T(8,128)}) custom-call(bf16[128,2048]{1,0:T(8,128)(2,1)} %get-tuple-element.10.refs_0_, bf16[128,2048]{1,0:T(8,128)(2,1)} %get-tuple-element.11.refs_1_, ...), custom_call_target="tpu_custom_call" | custom-call | tf_op jit(solution)/shard_map/pallas_call | solution.py:468

commit v2 on v1

--- a/solution.py
+++ b/solution.py
@@ -39,22 +39,38 @@
     return jnp.concatenate(parts, axis=0)
 
 
-def filter_tile(before, own, grads, mirror, groups, group_size):
+def filter_tile(before, own, turned, groups, group_size):
     tile, kernel = own.shape
     half = kernel // 2
     window = jnp.concatenate([before, own], axis=1)
     later = jnp.concatenate([window[:, half:], window[:, :half]], axis=1)
     data = jnp.concatenate([window, later], axis=0)
-    turned = dot(mirror, grads.T).astype(bf16)
     turned = jnp.concatenate([turned[:half], turned[half:]], axis=1)
     owner = lax.rem(iota((half, 2 * tile), 1), tile) // group_size
+    parts = dot(jnp.concatenate([turned * as_mask(owner == g) for g in range(groups)], axis=0), data)
     now = iota((half, kernel), 0) + iota((half, kernel), 1) <= half - 1
     rows = []
     for g in range(groups):
-        part = dot(turned * as_mask(owner == g), data)
+        part = parts[g * half : (g + 1) * half]
         square = jnp.where(now, part[:, kernel:], part[:, :kernel])
         rows.append(jnp.sum(fanned(square), axis=0, keepdims=True))
     return jnp.concatenate(rows, axis=0)
+
+
+def each(count, body):
+    if count <= 4:
+        for i in range(count):
+            body(i)
+    else:
+        pl.loop(0, count)(body)
+
+
+def when(condition, action):
+    if isinstance(condition, bool):
+        if condition:
+            action()
+    else:
+        pl.when(condition)(action)
 
 
 def kernel(
@@ -156,58 +172,78 @@
             at = tile_of(h, i)
             cot_t[at, :] = cot_ref[:, at].T
 
+    def kv_copy(h):
+        return remote(
+            kv_t.at[span(h)], rim_t.at[span(h)], kv_send.at[h], kv_recv.at[h], tok=lax.rem(tok + 1, n_tok)
+        )
+
+    def gc_copy(h):
+        return remote(
+            gc_t.at[span(h)], gcn_t.at[span(h)], gc_send.at[h], gc_recv.at[h], tok=lax.rem(tok + n_tok - 1, n_tok)
+        )
+
+    def sib_copy(p, h):
+        sem = p * pieces + h
+        return remote(
+            sib_out.at[p, span(h)], sib_in.at[p, span(h)], sib_send.at[sem], sib_recv.at[sem], wid=sibling
+        )
+
+    def pre_copy(p, slot, h):
+        return remote(
+            pre_out.at[p, span(h)], pre_in.at[slot, span(h)],
+            pre_send.at[p * pieces + h], pre_recv.at[slot * pieces + h], wid=p * 2 + core,
+        )
+
+    def send_sum(i):
+        p, h = step_of(i)
+        sib_copy(p, h).wait_recv()
+        pre_out[p, span(h), :] = (part_t[span(h), :] + sib_in[p, span(h), :].astype(f32)).astype(bf16)
+        pre_copy(p, chip, h).start()
+
+    def two_parts(i):
+        p, h = step_of(i)
+        w_copy(p * 2 + 1 - core, h).wait()
+        w_copy(p * 2 + core, h).wait()
+        sib_out[p, span(h), :] = dot(w_buf[w_rows(p * 2 + 1 - core, h), :], cot_t[...]).astype(bf16)
+        part_t[span(h), :] = dot(w_buf[w_rows(p * 2 + core, h), :], cot_t[...])
+
+    def own_parts(block, store):
+        for h in range(pieces):
+            w_copy(block, h).wait()
+        size = 2 * piece if pieces % 2 == 0 else piece
+        for start in range(0, width, size):
+            rows_at = pl.ds(pl.multiple_of(block * width + start, size), size)
+            store(pl.ds(start, size), dot(w_buf[rows_at, :], cot_t[...]))
+
+    two_parts(0)
     pl.semaphore_wait(barrier, 1 + len(other_chips) + len(other_toks))
-
-    def kv_copy(h):
-        return remote(
-            kv_t.at[span(h)], rim_t.at[span(h)], kv_send.at[h], kv_recv.at[h], tok=lax.rem(tok + 1, n_tok)
-        )
-
-    def gc_copy(h):
-        return remote(
-            gc_t.at[span(h)], gcn_t.at[span(h)], gc_send.at[h], gc_recv.at[h], tok=lax.rem(tok + n_tok - 1, n_tok)
-        )
+    sib_copy(*step_of(0)).start()
 
     @pl.when(has_next)
     def _():
         for h in range(pieces):
             kv_copy(h).start()
 
-    def sib_copy(p, h):
-        sem = p * pieces + h
-        return remote(
-            sib_out.at[p, span(h)], sib_in.at[p, span(h)], sib_send.at[sem], sib_recv.at[sem], wid=sibling
-        )
-
-    def pre_copy(p, slot, h):
-        return remote(
-            pre_out.at[p, span(h)], pre_in.at[slot, span(h)],
-            pre_send.at[p * pieces + h], pre_recv.at[slot * pieces + h], wid=p * 2 + core,
-        )
-
-    def grad_rows(block, h):
-        w_copy(block, h).wait()
-        return dot(w_buf[w_rows(block, h), :], cot_t[...])
-
-    def send_sum(i):
-        p, h = step_of(i)
-        sib_copy(p, h).wait_recv()
-        pre_out[p, span(h), :] = (part_t[span(h), :] + sib_in[p, span(h), :].astype(f32)).astype(bf16)
-        pre_copy(p, chip, h).start()
-
-    @pl.loop(0, steps)
-    def _(i):
-        p, h = step_of(i)
-        sib_out[p, span(h), :] = grad_rows(p * 2 + 1 - core, h).astype(bf16)
-        sib_copy(p, h).start()
-        pl.when(i > 0)(lambda: send_sum(i - 1))
-        part_t[span(h), :] = grad_rows(p * 2 + core, h)
-
-    @pl.loop(0, pieces)
-    def _(h):
-        sib_out[chip, span(h), :] = grad_rows(sibling, h).astype(bf16)
+    def sum_step(j):
+        i = j + 1
+        if pieces > 1:
+            two_parts(i)
+            sib_copy(*step_of(i)).start()
+            send_sum(i - 1)
+        else:
+            send_sum(i - 1)
+            two_parts(i)
+            sib_copy(*step_of(i)).start()
+
+    each(steps - 1, sum_step)
+
+    def store_sibling(at, product):
+        sib_out[chip, at, :] = product.astype(bf16)
+
+    own_parts(sibling, store_sibling)
+    for h in range(pieces):
         sib_copy(chip, h).start()
-        pl.when(h == 0)(lambda: send_sum(steps - 1))
+    send_sum(steps - 1)
 
     ins[3].wait()
     ins[4].wait()
@@ -253,10 +289,13 @@
             peer_copy(p, h, me, chip).start()
         own_copy(h, me).start()
 
-    @pl.loop(0, pieces)
-    def _(h):
+    def store_own(at, product):
+        part_t[at, :] = product
+
+    forward_piece(0)
+    own_parts(me, store_own)
+    for h in range(1, pieces - 1):
         forward_piece(h)
-        part_t[span(h), :] = grad_rows(me, h)
 
     mirror = as_mask(
         jnp.logical_and(
@@ -265,28 +304,36 @@
         )
     )
 
-    @pl.loop(0, pieces)
-    def _(h):
+    def backward_piece(h):
         sib_copy(chip, h).wait_recv()
         for p in other_chips:
             pre_copy(p, p, h).wait_recv()
+        turned = []
         for i in range(tiles):
             at = tile_of(h, i)
             grad_gated = part_t[at, :] + sib_in[chip, at, :].astype(f32)
             for p in other_chips:
                 grad_gated = grad_gated + pre_in[p, at, :].astype(f32)
-            gc_t[at, :] = (grad_gated * q_t[at, :].astype(f32)).astype(bf16)
+            grad_conv = (grad_gated * q_t[at, :].astype(f32)).astype(bf16)
+            gc_t[at, :] = grad_conv
+            turned.append(grad_conv.T)
             gq_buf[:, at] = (grad_gated * conv_t[at, :]).astype(bf16).T
 
         @pl.when(has_previous)
         def _():
             gc_copy(h).start()
 
+        turned = dot(mirror, jnp.concatenate(turned, axis=1)).astype(bf16)
         for i in range(tiles):
             at = tile_of(h, i)
             local_buf[groups_of(h, i), :] = filter_tile(
-                rim_t[at, :], kv_t[at, :], gc_t[at, :], mirror, tile_groups, group_size
+                rim_t[at, :], kv_t[at, :], turned[:, i * tile : (i + 1) * tile], tile_groups, group_size
             )
+
+    for h in range(pieces):
+        if h == pieces // 2 and pieces > 1:
+            forward_piece(pieces - 1)
+        backward_piece(h)
 
     outs = [
         pltpu.make_async_copy(src, dst, out_sem.at[i])
@@ -318,15 +365,14 @@
     for t in other_toks:
         if_owner(t, lambda t=t: term_copy(t, tok).start())
 
-    def project(block, start, depth, first=False):
+    def project(block, start, depth):
         deep = pl.ds(pl.multiple_of(block * width + start, depth), depth)
-        product = dot(gather[block, :, pl.ds(pl.multiple_of(start, depth), depth)], w_buf[deep, :])
-        total[...] = product if first else total[...] + product
-
-    project(me, 0, width, True)
+        return dot(gather[block, :, pl.ds(pl.multiple_of(start, depth), depth)], w_buf[deep, :])
+
     for h in range(pieces):
         own_copy(h, sibling).wait_recv()
-    project(sibling, 0, width)
+    both = pl.ds(pl.multiple_of(chip * 2 * width, 2 * width), 2 * width)
+    total[...] = dot(jnp.concatenate([gather[chip * 2], gather[chip * 2 + 1]], axis=1), w_buf[both, :])
 
     def sum_terms():
         for t in other_toks:
@@ -358,21 +404,29 @@
     outs[1].start()
     outs[2].start()
 
-    def last_half(i):
-        p, h = step_of(i)
-        fwd_copy(p, h, p * 2 + 1 - core).wait_recv()
-        project(p * 2 + 1 - core, h * piece, piece)
-
-    @pl.loop(0, steps)
-    def _(i):
+    def arrived(i):
         p, h = step_of(i)
         peer_copy(p, h, p * 2 + core, p).wait_recv()
         fwd_copy(p, h, p * 2 + core).start()
-        pl.when(i > 0)(lambda: last_half(i - 1))
-        project(p * 2 + core, h * piece, piece)
-
-    last_half(steps - 1)
-    out_buf[...] = total[...].astype(bf16)
+
+    def near_half(i):
+        p, h = step_of(i)
+        return project(p * 2 + core, h * piece, piece)
+
+    def far_half(i):
+        p, h = step_of(i)
+        fwd_copy(p, h, p * 2 + 1 - core).wait_recv()
+        return project(p * 2 + 1 - core, h * piece, piece)
+
+    arrived(0)
+    total[...] = total[...] + near_half(0)
+
+    def add_step(j):
+        arrived(j + 1)
+        total[...] = total[...] + (far_half(j) + near_half(j + 1))
+
+    each(steps - 1, add_step)
+    out_buf[...] = (total[...] + far_half(steps - 1)).astype(bf16)
     outs[3].start()
     for t in other_toks:
         if_owner(t, lambda t=t: sum_copy(t, t).wait_recv())
@@ -405,12 +459,17 @@
 
 
 def hand_on(*refs):
-    count = len(refs) // 2
-    sems = refs[-1]
-    copies = [pltpu.make_async_copy(refs[i], refs[count + i], sems.at[i]) for i in range(count)]
-    for copy in copies:
+    count = (len(refs) - 2) // 3
+    source, target, held = refs[:count], refs[count : 2 * count], refs[2 * count : 3 * count]
+    in_sem, out_sem = refs[3 * count :]
+    loads = [pltpu.make_async_copy(source[i], held[i], in_sem.at[i]) for i in range(count)]
+    stores = [pltpu.make_async_copy(held[i], target[i], out_sem.at[i]) for i in range(count)]
+    for copy in loads:
         copy.start()
-    for copy in copies:
+    for load, store in zip(loads, stores):
+        load.wait()
+        store.start()
+    for copy in stores:
         copy.wait()
 
 
@@ -466,7 +525,7 @@
         ),
     )(queries, key_branch, value_branch, filters, out_weight, cotangent)
     return pl.pallas_call(
-        hand_on, in_specs=[hbm] * 5, out_specs=[hbm] * 5, out_shape=results, scratch_shapes=[dma((5,))]
+        hand_on, in_specs=[hbm] * 5, out_specs=[hbm] * 5, out_shape=results, scratch_shapes=[flat] * 4 + [taps, dma((5,)), dma((5,))]
     )(*outs)
 
 

time: 115 us -> 46 us (0.40)
  Pallas kernels: 114 us -> 45 us
    pallas_call x1, Pallas kernels: 66.7 us -> 2.45 us  [local(): pl.pallas_call(hand_on, in_specs=[hbm] * 5, out_specs=[hbm] * 5, out_shap...]
    pallas_call x1, Pallas kernels: 47.5 us -> 42.5 us  [local(): pl.pallas_call(functools.partial(kernel, (n_tok, n_wid, tile, piece, owne...]
where the time goes in v2:
time: 46 us; the launch traced here: 45.8 us
  Pallas kernels  45 us (98%)
  between operations  0.82 us (2%)
    pallas_call x1, Pallas kernels, local(): pl.pallas_call(functools.partial(kernel, (n_tok, n_wid, tile, piece, owne...  42.5 us
    pallas_call x1, Pallas kernels, local(): pl.pallas_call(hand_on, in_specs=[hbm] * 5, out_specs=[hbm] * 5, out_shap...  2.45 us

profile of v2, /device:TPU:0, one launch (start us, length us, event | category | flops | bytes accessed | tf_op | source)
XLA Modules:
  0.0 45.8 jit_solution(918330613483019926)
XLA Ops:
  0.6 42.5 %shard_map.101 = (bf16[128,2048]{1,0:T(8,128)(2,1)}, bf16[128,2048]{1,0:T(8,128)(2,1)}, bf16[128,2048]{1,0:T(8,128)(2,1)}, bf16[128,2048]{1,0:T(8,128)(2,1)}, f32[128,128]{1,0:T(8,128)}) custom-call(bf16[128,2048]{1,0:T(8,128)(2,1)} %q_hbm.1, bf16[128,2048]{1,0:T(8,128)(2,1)} %k_hbm.1, bf16[128,2048]{1,0:T(8,128)(2,1)} %v_hbm.1, f32[128,128]{1,0:T(8,128)} %f_hbm.1, ...), custom_call_target="tpu_custom_call" | custom-call | flops 8589934592 | bytes 33554432 | tf_op jit(solution)/shard_map/pallas_call | solution.py:495
  43.2 2.4 %shard_map.102 = (bf16[128,2048]{1,0:T(8,128)(2,1)}, bf16[128,2048]{1,0:T(8,128)(2,1)}, bf16[128,2048]{1,0:T(8,128)(2,1)}, bf16[128,2048]{1,0:T(8,128)(2,1)}, f32[128,128]{1,0:T(8,128)}) custom-call(bf16[128,2048]{1,0:T(8,128)(2,1)} %get-tuple-element.10.refs_0_, bf16[128,2048]{1,0:T(8,128)(2,1)} %get-tuple-element.11.refs_1_, ...), custom_call_target="tpu_custom_call" | custom-call | tf_op jit(solution)/shard_map/pallas_call | solution.py:527

commit v3 on v2

--- a/solution.py
+++ b/solution.py
@@ -172,6 +172,11 @@
             at = tile_of(h, i)
             cot_t[at, :] = cot_ref[:, at].T
 
+    def turn_queries():
+        for i in range(width // tile):
+            at = pl.ds(i * tile, tile)
+            q_t[at, :] = q_ref[:, at].T
+
     def kv_copy(h):
         return remote(
             kv_t.at[span(h)], rim_t.at[span(h)], kv_send.at[h], kv_recv.at[h], tok=lax.rem(tok + 1, n_tok)
@@ -215,14 +220,15 @@
             rows_at = pl.ds(pl.multiple_of(block * width + start, size), size)
             store(pl.ds(start, size), dot(w_buf[rows_at, :], cot_t[...]))
 
-    two_parts(0)
     pl.semaphore_wait(barrier, 1 + len(other_chips) + len(other_toks))
-    sib_copy(*step_of(0)).start()
 
     @pl.when(has_next)
     def _():
         for h in range(pieces):
             kv_copy(h).start()
+
+    two_parts(0)
+    sib_copy(*step_of(0)).start()
 
     def sum_step(j):
         i = j + 1
@@ -280,11 +286,9 @@
         keep = as_mask(sublanes <= lanes)
         for i in range(tiles):
             at = tile_of(h, i)
-            turned = q_ref[:, at].T
             conv = conv_tile(f_ref[groups_of(h, i), :], kv_t[at, :], rim_t[at, :], keep, group_size)
-            q_t[at, :] = turned
             conv_t[at, :] = conv
-            gather[me, :, at] = (turned.astype(f32) * conv).astype(bf16).T
+            gather[me, :, at] = (q_t[at, :].astype(f32) * conv).astype(bf16).T
         for p in other_chips:
             peer_copy(p, h, me, chip).start()
         own_copy(h, me).start()
@@ -292,10 +296,8 @@
     def store_own(at, product):
         part_t[at, :] = product
 
-    forward_piece(0)
+    turn_queries()
     own_parts(me, store_own)
-    for h in range(1, pieces - 1):
-        forward_piece(h)
 
     mirror = as_mask(
         jnp.logical_and(
@@ -304,25 +306,29 @@
         )
     )
 
-    def backward_piece(h):
+    def grad_piece(h):
         sib_copy(chip, h).wait_recv()
         for p in other_chips:
             pre_copy(p, p, h).wait_recv()
+        at = span(h)
+        grad_gated = part_t[at, :] + sib_in[chip, at, :].astype(f32)
+        for p in other_chips:
+            grad_gated = grad_gated + pre_in[p, at, :].astype(f32)
+        gc_t[at, :] = (grad_gated * q_t[at, :].astype(f32)).astype(bf16)
+        part_t[at, :] = grad_gated
+
+    def send_grads(which):
+        @pl.when(has_previous)
+        def _():
+            for h in which:
+                gc_copy(h).start()
+
+    def filter_piece(h):
         turned = []
         for i in range(tiles):
             at = tile_of(h, i)
-            grad_gated = part_t[at, :] + sib_in[chip, at, :].astype(f32)
-            for p in other_chips:
-                grad_gated = grad_gated + pre_in[p, at, :].astype(f32)
-            grad_conv = (grad_gated * q_t[at, :].astype(f32)).astype(bf16)
-            gc_t[at, :] = grad_conv
-            turned.append(grad_conv.T)
-            gq_buf[:, at] = (grad_gated * conv_t[at, :]).astype(bf16).T
-
-        @pl.when(has_previous)
-        def _():
-            gc_copy(h).start()
-
+            gq_buf[:, at] = (part_t[at, :] * conv_t[at, :]).astype(bf16).T
+            turned.append(gc_t[at, :].T)
         turned = dot(mirror, jnp.concatenate(turned, axis=1)).astype(bf16)
         for i in range(tiles):
             at = tile_of(h, i)
@@ -331,9 +337,14 @@
             )
 
     for h in range(pieces):
-        if h == pieces // 2 and pieces > 1:
-            forward_piece(pieces - 1)
-        backward_piece(h)
+        forward_piece(h)
+    first = max(pieces - 2, 0)
+    for h in range(pieces):
+        grad_piece(h)
+        if h < first:
+            send_grads([h])
+    for h in range(pieces):
+        filter_piece(h)
 
     outs = [
         pltpu.make_async_copy(src, dst, out_sem.at[i])
@@ -364,6 +375,7 @@
 
     for t in other_toks:
         if_owner(t, lambda t=t: term_copy(t, tok).start())
+    send_grads(range(first, pieces))
 
     def project(block, start, depth):
         deep = pl.ds(pl.multiple_of(block * width + start, depth), depth)
@@ -382,14 +394,12 @@
         for t in other_toks:
             sum_copy(t, tok).start()
 
-    if_owner(tok, sum_terms)
 
     @pl.when(jnp.logical_not(has_next))
     def _():
         gcn_t[...] = jnp.zeros_like(gcn_t)
 
-    @pl.loop(0, pieces)
-    def _(h):
+    def back_piece(h):
         @pl.when(has_next)
         def _():
             gc_copy(h).wait_recv()
@@ -401,31 +411,44 @@
             gk_buf[:, at] = (grad_kv * v_ref[:, at].astype(f32)).astype(bf16)
             gv_buf[:, at] = (grad_kv * k_ref[:, at].astype(f32)).astype(bf16)
 
+    def arrived(i):
+        p, h = step_of(i)
+        peer_copy(p, h, p * 2 + core, p).wait_recv()
+        fwd_copy(p, h, p * 2 + core).start()
+
+    def near_half(i):
+        p, h = step_of(i)
+        return project(p * 2 + core, h * piece, piece)
+
+    def far_half(i):
+        p, h = step_of(i)
+        fwd_copy(p, h, p * 2 + 1 - core).wait_recv()
+        return project(p * 2 + 1 - core, h * piece, piece)
+
+    mixed = steps == pieces
+    back_piece(0)
+    arrived(0)
+    total[...] = total[...] + near_half(0)
+
+    def add_step(j):
+        if mixed:
+            back_piece(j + 1)
+        arrived(j + 1)
+        total[...] = total[...] + (far_half(j) + near_half(j + 1))
+
+    if not mixed:
+        for h in range(1, pieces):
+            back_piece(h)
+    early = max(steps - 3, 0) if mixed else 0
+    each(early, add_step)
+    if_owner(tok, sum_terms)
+    if mixed:
+        for j in range(early, steps - 1):
+            add_step(j)
+    else:
+        each(steps - 1, add_step)
     outs[1].start()
     outs[2].start()
-
-    def arrived(i):
-        p, h = step_of(i)
-        peer_copy(p, h, p * 2 + core, p).wait_recv()
-        fwd_copy(p, h, p * 2 + core).start()
-
-    def near_half(i):
-        p, h = step_of(i)
-        return project(p * 2 + core, h * piece, piece)
-
-    def far_half(i):
-        p, h = step_of(i)
-        fwd_copy(p, h, p * 2 + 1 - core).wait_recv()
-        return project(p * 2 + 1 - core, h * piece, piece)
-
-    arrived(0)
-    total[...] = total[...] + near_half(0)
-
-    def add_step(j):
-        arrived(j + 1)
-        total[...] = total[...] + (far_half(j) + near_half(j + 1))
-
-    each(steps - 1, add_step)
     out_buf[...] = (total[...] + far_half(steps - 1)).astype(bf16)
     outs[3].start()
     for t in other_toks:

time: 46 us -> 40.6 us (0.88)
  Pallas kernels: 45 us -> 39.4 us
    pallas_call x1, Pallas kernels: 42.5 us -> 36.9 us  [local(): pl.pallas_call(functools.partial(kernel, (n_tok, n_wid, tile, piece, owne...]
where the time goes in v3:
time: 40.6 us; the launch traced here: 40.2 us
  Pallas kernels  39.4 us (97%)
  between operations  0.82 us (2%)
    pallas_call x1, Pallas kernels, local(): pl.pallas_call(functools.partial(kernel, (n_tok, n_wid, tile, piece, owne...  36.9 us
    pallas_call x1, Pallas kernels, local(): pl.pallas_call(hand_on, in_specs=[hbm] * 5, out_specs=[hbm] * 5, out_shap...  2.45 us

profile of v3, /device:TPU:0, one launch (start us, length us, event | category | flops | bytes accessed | tf_op | source)
XLA Modules:
  0.0 40.2 jit_solution(15618519041463018233)
XLA Ops:
  0.6 36.9 %shard_map.101 = (bf16[128,2048]{1,0:T(8,128)(2,1)}, bf16[128,2048]{1,0:T(8,128)(2,1)}, bf16[128,2048]{1,0:T(8,128)(2,1)}, bf16[128,2048]{1,0:T(8,128)(2,1)}, f32[128,128]{1,0:T(8,128)}) custom-call(bf16[128,2048]{1,0:T(8,128)(2,1)} %q_hbm.1, bf16[128,2048]{1,0:T(8,128)(2,1)} %k_hbm.1, bf16[128,2048]{1,0:T(8,128)(2,1)} %v_hbm.1, f32[128,128]{1,0:T(8,128)} %f_hbm.1, ...), custom_call_target="tpu_custom_call" | custom-call | flops 8589934592 | bytes 33554432 | tf_op jit(solution)/shard_map/pallas_call | solution.py:518
  37.6 2.4 %shard_map.102 = (bf16[128,2048]{1,0:T(8,128)(2,1)}, bf16[128,2048]{1,0:T(8,128)(2,1)}, bf16[128,2048]{1,0:T(8,128)(2,1)}, bf16[128,2048]{1,0:T(8,128)(2,1)}, f32[128,128]{1,0:T(8,128)}) custom-call(bf16[128,2048]{1,0:T(8,128)(2,1)} %get-tuple-element.10.refs_0_, bf16[128,2048]{1,0:T(8,128)(2,1)} %get-tuple-element.11.refs_1_, ...), custom_call_target="tpu_custom_call" | custom-call | tf_op jit(solution)/shard_map/pallas_call | solution.py:550

commit v4 on v3

--- a/solution.py
+++ b/solution.py
@@ -336,11 +336,13 @@
                 rim_t[at, :], kv_t[at, :], turned[:, i * tile : (i + 1) * tile], tile_groups, group_size
             )
 
-    for h in range(pieces):
+    first = max(pieces - 2, 0)
+    for h in range(pieces - 1):
         forward_piece(h)
-    first = max(pieces - 2, 0)
     for h in range(pieces):
         grad_piece(h)
+        if h == 0:
+            forward_piece(pieces - 1)
         if h < first:
             send_grads([h])
     for h in range(pieces):

time: 40.6 us -> 40.6 us (level)
  no operation moved by 1% of the time
where the time goes in v4:
time: 40.6 us; the launch traced here: 40.2 us
  Pallas kernels  39.4 us (97%)
  between operations  0.82 us (2%)
    pallas_call x1, Pallas kernels, local(): pl.pallas_call(functools.partial(kernel, (n_tok, n_wid, tile, piece, owne...  36.9 us
    pallas_call x1, Pallas kernels, local(): pl.pallas_call(hand_on, in_specs=[hbm] * 5, out_specs=[hbm] * 5, out_shap...  2.45 us

profile of v4, /device:TPU:0, one launch (start us, length us, event | category | flops | bytes accessed | tf_op | source)
XLA Modules:
  0.0 40.2 jit_solution(2539627288968604917)
XLA Ops:
  0.6 36.9 %shard_map.101 = (bf16[128,2048]{1,0:T(8,128)(2,1)}, bf16[128,2048]{1,0:T(8,128)(2,1)}, bf16[128,2048]{1,0:T(8,128)(2,1)}, bf16[128,2048]{1,0:T(8,128)(2,1)}, f32[128,128]{1,0:T(8,128)}) custom-call(bf16[128,2048]{1,0:T(8,128)(2,1)} %q_hbm.1, bf16[128,2048]{1,0:T(8,128)(2,1)} %k_hbm.1, bf16[128,2048]{1,0:T(8,128)(2,1)} %v_hbm.1, f32[128,128]{1,0:T(8,128)} %f_hbm.1, ...), custom_call_target="tpu_custom_call" | custom-call | flops 8589934592 | bytes 33554432 | tf_op jit(solution)/shard_map/pallas_call | solution.py:520
  37.6 2.4 %shard_map.102 = (bf16[128,2048]{1,0:T(8,128)(2,1)}, bf16[128,2048]{1,0:T(8,128)(2,1)}, bf16[128,2048]{1,0:T(8,128)(2,1)}, bf16[128,2048]{1,0:T(8,128)(2,1)}, f32[128,128]{1,0:T(8,128)}) custom-call(bf16[128,2048]{1,0:T(8,128)(2,1)} %get-tuple-element.10.refs_0_, bf16[128,2048]{1,0:T(8,128)(2,1)} %get-tuple-element.11.refs_1_, ...), custom_call_target="tpu_custom_call" | custom-call | tf_op jit(solution)/shard_map/pallas_call | solution.py:552
